TPU v7x, 256 devices: a whole 4x4x8 slice. The times are simulated.
256 devices in a mesh: seg: 32 (over x, z), term: 8 (over y, core).
Axes of the slice: x: 4, y: 4, z: 8, core: 2. Of those that a mesh axis runs over, the one named last changes fastest.
Arguments:
- left_blocks: bfloat16 [32, 32, 512, 512], P('seg', 'term'), may hold values from -0.25 to 0.25
- right_blocks: bfloat16 [32, 32, 512, 512], P('seg', 'term'), may hold values from -0.046875 to 0.046875
- start_state: float32 [32, 512, 512], P('seg'), may hold values from -6 to 6
- left_transfer: float32 [32, 512, 512], P('seg'), as said below
- right_transfer: float32 [32, 512, 512], P('seg'), as said below
- ranks: int32 [32, 2], P('seg'), may hold values from 128 to 512
Outputs:
- final_state: float32 [32, 512, 512], P('seg')
Inputs may be any that keep to these rules, and one draw needn't show every extreme that they name: `left_transfer`: entries of size about 0.3 / sqrt(512). `right_transfer`: entries of size about 0.3 / sqrt(512).
All inputs are finite; a program needn't handle non-finite values.
Results may differ from a plain program's by a relative error of at most 0.008.
Values may be sent and summed in bfloat16 or wider, within the bound.
A program may use at most 128 MiB of HBM per device.

v0:
```python
import jax
import jax.numpy as jnp
from jax import lax
from jax.sharding import PartitionSpec as P

ITERS = 2


def prefix(part, axis, combine, identity, reverse):
    count = lax.axis_size(axis)
    place = lax.axis_index(axis)
    ahead = count - 1 - place if reverse else place
    gathered = lax.all_gather(part, axis)
    state = jnp.zeros_like(part) + jnp.asarray(identity, part.dtype)

    def one(lap, state):
        source = count - 1 - lap if reverse else lap
        return combine(state, lax.dynamic_index_in_dim(gathered, source, 0, False))

    return lax.fori_loop(0, ahead, one, state)


def passed_along(shard, axis, by):
    length = lax.axis_size(axis)
    pairs = [(i, i + by) for i in range(length) if 0 <= i + by < length]
    return lax.ppermute(shard, axis, pairs)


def normed(block, target):
    return block * (target / jnp.sqrt(jnp.sum(block * block) + 1e-06))


def combine_env(earlier, later):
    root = float(earlier.shape[0]) ** 0.5
    return normed(jnp.dot(earlier, later, precision=lax.Precision.HIGHEST), root)


def term_partial(left_ops, right_ops, moved):
    inner = jnp.einsum("tij,jk->tik", left_ops, moved, preferred_element_type=jnp.float32).astype(
        jnp.bfloat16
    )
    return jnp.einsum("tik,tlk->il", inner, right_ops, preferred_element_type=jnp.float32)


def half_sweep(left_ops, right_ops, basis, start, live_mask):
    block_size = start.shape[0]
    basis_b = basis.astype(jnp.bfloat16)
    basis_wide = basis_b.astype(jnp.float32)
    state = normed(start * live_mask, float(block_size))
    for step_index in range(ITERS):
        state_b = state.astype(jnp.bfloat16)
        moved = jnp.dot(basis_b, state_b, preferred_element_type=jnp.float32).astype(jnp.bfloat16)
        partial_sum = term_partial(left_ops, right_ops, moved)
        term_total = lax.psum(partial_sum, "term")
        applied = lax.dot_general(
            basis_wide, term_total, (((0,), (0,)), ((), ())), precision=lax.Precision.HIGHEST
        )
        state = normed((2.0 * state - applied) * live_mask, float(block_size))
    return state


def per_device(left_blocks, right_blocks, start_state, left_transfer, right_transfer, ranks):
    block_size = start_state.shape[-1]
    unit_matrix = jnp.eye(block_size, dtype=jnp.float32)
    root = float(block_size) ** 0.5
    left_unit = normed(unit_matrix + left_transfer[0], root)
    right_unit = normed(unit_matrix + right_transfer[0], root)
    left_env = prefix(left_unit, "seg", combine_env, unit_matrix, False)
    right_env = prefix(right_unit, "seg", combine_env, unit_matrix, True)
    positions = jnp.arange(block_size)
    rows_live = (positions < ranks[0, 0]).astype(jnp.float32)
    cols_live = (positions < ranks[0, 1]).astype(jnp.float32)
    live_mask = rows_live[:, None] * cols_live[None, :]
    first_state = half_sweep(left_blocks[0], right_blocks[0], left_env, start_state[0], live_mask)
    neighbour = passed_along(first_state.astype(jnp.bfloat16), "seg", 1)
    seeded = first_state + 0.5 * neighbour.astype(jnp.float32)
    flipped = half_sweep(right_blocks[0], left_blocks[0], right_env.T, seeded.T, live_mask.T)
    return flipped.T[None]


def solution(mesh):
    in_specs = (
        P("seg", "term", None, None),
        P("seg", "term", None, None),
        P("seg", None, None),
        P("seg", None, None),
        P("seg", None, None),
        P("seg", None),
    )
    out_specs = P("seg", None, None)
    return jax.shard_map(
        per_device, mesh=mesh, in_specs=in_specs, out_specs=out_specs, check_vma=False
    )
```

profile of v0, /device:TPU:2, one launch (start us, length us, event | category | flops | bytes accessed | tf_op | source)
XLA Modules:
  0.0 1196.1 jit_solution(1782328151539934472)
XLA Ops:
  6.5 2.7 copy.19
  20.8 227.6 %all-gather.3.cloned.1.call-done = f32[32,512,512]{2,1,0:T(8,128)} async-done(((f32[1,512,512]{2,1,0:T(8,128)}), f32[32,512,512]{2,1,0:T(8,128)}) %all-gather.3.cloned.1.call-update) | async-done | bytes 33554448 | tf_op jit(solution)/shard_map/all_gather | solution.py:13
  248.4 47.2 %while.22 = (s32[]{:T(128)}, f32[512,512]{0,1:T(8,128)}, s32[]{:T(128)}, f32[32,512,512]{2,1,0:T(8,128)}, s32[]{:T(128)}, /*index=5*/s32[]{:T(128)}, s32[]{:T(128)}, f32[]{:T(128)}, f32[]{:T(128)}) while((s32[]{:T(128)}, f32[512,512]{0,1:T(8,128)}, s32[]{:T(128)}, f32[32,512,512]{2,1,0:T(8,128)}, s32[]{:T(128)}, /*index=5*/s32[]{:T(128)}, ...), condition=%wide.region_4.5_spmd, body=%wide.region_2.4_spmd.sunk | while | flops 1611399168 | bytes 5243051 | solution.py:20
  248.4 4.1 multiply_reduce_fusion.9
  254.3 4.2 multiply_reduce_fusion.9
  260.2 4.1 multiply_reduce_fusion.9
  266.1 4.2 multiply_reduce_fusion.9
  272.0 4.1 multiply_reduce_fusion.9
  277.9 4.2 multiply_reduce_fusion.9
  283.8 4.1 multiply_reduce_fusion.9
  289.7 4.2 multiply_reduce_fusion.9
  296.9 5.2 fusion.28
  302.1 3.2 copy.64
  305.4 2.4 fusion.50
  311.1 2.5 copy.20
  313.6 193.5 %all-reduce.5.cloned.1.call-done = f32[512,512]{1,0:T(8,128)} async-done(((f32[512,512]{1,0:T(8,128)}), f32[512,512]{1,0:T(8,128)}) %all-reduce.5.cloned.1.call-update) | async-done | bytes 1048592 | tf_op jit(solution)/shard_map/psum | solution.py:54
  507.2 4.4 multiply_reduce_fusion.5
  512.3 5.1 fusion.31
  517.4 3.2 copy.63
  520.6 2.3 fusion.55
  523.0 2.5 copy.25
  528.5 2.3 fusion.67
  530.9 59.2 %all-reduce.7.cloned.1.call-done = f32[512,512]{1,0:T(8,128)} async-done(((f32[512,512]{1,0:T(8,128)}), f32[512,512]{1,0:T(8,128)}) %all-reduce.7.cloned.1.call-update) | async-done | bytes 1048592 | tf_op jit(solution)/shard_map/psum | solution.py:54
  590.1 4.4 multiply_reduce_fusion.4
  597.3 3.5 collective-permute-start
  600.8 228.4 %all-gather.5.cloned.1.call-done = f32[32,512,512]{2,1,0:T(8,128)} async-done(((f32[1,512,512]{2,1,0:T(8,128)}), f32[32,512,512]{2,1,0:T(8,128)}) %all-gather.5.cloned.1.call-update) | async-done | bytes 33554448 | tf_op jit(solution)/shard_map/all_gather | solution.py:13
  829.2 134.0 %while.23 = (s32[]{:T(128)}, f32[512,512]{0,1:T(8,128)}, s32[]{:T(128)}, f32[32,512,512]{2,1,0:T(8,128)}, s32[]{:T(128)}, /*index=5*/s32[]{:T(128)}, s32[]{:T(128)}, s32[]{:T(128)}, f32[]{:T(128)}, f32[]{:T(128)}) while((s32[]{:T(128)}, f32[512,512]{0,1:T(8,128)}, s32[]{:T(128)}, f32[32,512,512]{2,1,0:T(8,128)}, s32[]{:T(128)}, ...), condition=%wide.region_13.14_spmd, body=%wide.region_11.13_spmd.sunk | while | flops 1611399168 | bytes 5243071 | solution.py:20
  829.2 4.1 multiply_reduce_fusion.10
  835.1 4.1 multiply_reduce_fusion.10
  840.9 4.1 multiply_reduce_fusion.10
  846.7 4.1 multiply_reduce_fusion.10
  852.5 4.1 multiply_reduce_fusion.10
  858.4 4.1 multiply_reduce_fusion.10
  864.2 4.1 multiply_reduce_fusion.10
  870.0 4.1 multiply_reduce_fusion.10
  875.8 4.1 multiply_reduce_fusion.10
  881.7 4.1 multiply_reduce_fusion.10
  887.5 4.1 multiply_reduce_fusion.10
  893.3 4.1 multiply_reduce_fusion.10
  899.1 4.1 multiply_reduce_fusion.10
  905.0 4.1 multiply_reduce_fusion.10
  910.8 4.1 multiply_reduce_fusion.10
  916.6 4.1 multiply_reduce_fusion.10
  922.4 4.1 multiply_reduce_fusion.10
  928.3 4.1 multiply_reduce_fusion.10
  934.1 4.1 multiply_reduce_fusion.10
  939.9 4.1 multiply_reduce_fusion.10
  945.7 4.1 multiply_reduce_fusion.10
  951.6 4.1 multiply_reduce_fusion.10
  957.4 4.1 multiply_reduce_fusion.10
  968.2 4.2 fusion.34
  972.3 3.4 copy.62
  978.0 109.2 %all-reduce.9.cloned.1.call-done = f32[512,512]{1,0:T(8,128)} async-done(((f32[512,512]{1,0:T(8,128)}), f32[512,512]{1,0:T(8,128)}) %all-reduce.9.cloned.1.call-update) | async-done | bytes 1048592 | tf_op jit(solution)/shard_map/psum | solution.py:54
  1087.2 3.4 fusion.102
  1090.7 2.5 copy.26
  1093.2 3.2 multiply_reduce_fusion.2
  1097.1 4.4 fusion.37
  1101.6 3.4 copy.61
  1108.6 65.8 %all-reduce.11.cloned.1.call-done = f32[512,512]{1,0:T(8,128)} async-done(((f32[512,512]{1,0:T(8,128)}), f32[512,512]{1,0:T(8,128)}) %all-reduce.11.cloned.1.call-update) | async-done | bytes 1048592 | tf_op jit(solution)/shard_map/psum | solution.py:54
  1174.4 3.5 fusion.103
  1177.8 2.7 copy.27
  1180.5 2.5 fusion.77
  1183.7 3.0 fusion.69
  1186.7 2.5 copy.28
  (84 shorter events, 62.6 us)
Async XLA Ops:
  6.5 298.8 %copy-start = (bf16[1,4,512,512]{3,2,1,0:T(8,128)(2,1)S(1)}, bf16[1,4,512,512]{3,2,1,0:T(8,128)(2,1)}, u32[]{:S(2)}) copy-start(bf16[1,4,512,512]{3,2,1,0:T(8,128)(2,1)} %param.11) | copy-start | bytes 6291460
  6.5 5.6 copy-start.7
  6.5 241.9 %all-gather.3.cloned.1.call-start = ((), (), s32[]{:S(2)}) async-start(), calls=%async_computation | async-start | bytes 34603008 | tf_op jit(solution)/shard_map/all_gather | solution.py:13
  13.3 1.6 copy-start.8
  13.3 493.8 %all-reduce.5.cloned.1.call-start = ((), (), s32[]{:S(2)}) async-start(), calls=%async_computation.1 | async-start | bytes 2097152 | tf_op jit(solution)/shard_map/psum | solution.py:54
  14.9 5.8 copy-start.3
  18.8 1.0 copy-start.1
  296.9 5.2 copy-start.6
  305.4 2.6 copy-start.4
  307.8 282.3 %all-reduce.7.cloned.1.call-start = ((), (), s32[]{:S(2)}) async-start(), calls=%async_computation.2 | async-start | bytes 2097152 | tf_op jit(solution)/shard_map/psum | solution.py:54
  523.0 306.2 %all-gather.5.cloned.1.call-start = ((), (), s32[]{:S(2)}) async-start(), calls=%async_computation.3 | async-start | bytes 34603008 | tf_op jit(solution)/shard_map/all_gather | solution.py:13
  530.9 556.4 %all-reduce.9.cloned.1.call-start = ((), (), s32[]{:S(2)}) async-start(), calls=%async_computation.4 | async-start | bytes 2097152 | tf_op jit(solution)/shard_map/psum | solution.py:54
  597.3 368.0 %collective-permute-start = (bf16[512,512]{1,0:T(8,128)(2,1)}, bf16[512,512]{1,0:T(8,128)(2,1)}, u32[]{:S(2)}, u32[]{:S(2)}) collective-permute-start(bf16[512,512]{1,0:T(8,128)(2,1)} %multiply_convert_fusion.2), channel_id=1, source_target_pairs={{0,8},{8,16},{16,24},{24,32},{32,40},{40,48},{48,56},{56,64},{64,7... | collective-permute-start | bytes 1572872 | tf_op jit(solution)/shard_map/ppermute | solution.py:26
  963.2 2.2 copy-start.2
  972.3 3.4 copy-start.9
  978.0 196.4 %all-reduce.11.cloned.1.call-start = ((), (), s32[]{:S(2)}) async-start(), calls=%async_computation.5 | async-start | bytes 2097152 | tf_op jit(solution)/shard_map/psum | solution.py:54
  1101.6 3.4 copy-start.10
  1177.8 5.9 copy-start.5
Sparse Core Ops, SparseCore 0:
  13.4 234.9 all-gather.2
  307.9 199.2 all-reduce.4
  523.1 66.9 all-reduce.6
  592.5 236.6 all-gather.4
  978.1 109.0 all-reduce.8
  1107.4 66.9 all-reduce.10
where the time goes:
time: 1200 us
  waiting for transfers between devices  884 us (74%)
  matrix products  172 us (14%)
  other arithmetic  61.5 us (5%)
  local copies, waits for them, and re-layouts  35.8 us (3%)
  loops' own time  19.7 us (2%)
  between operations  19.3 us (2%)
    all_gather x2, waiting for transfers between devices, prefix(): gathered = lax.all_gather(part, axis)  456 us
    psum x4, waiting for transfers between devices, half_sweep(): term_total = lax.psum(partial_sum, 'term')  428 us
    dot_general x31, matrix products, combine_env(): jnp.dot(earlier, later, precision=lax.Precision.HIGHEST)  128 us
    mul x33, other arithmetic, normed(): return block * (target / jnp.sqrt(jnp.sum(block * block) + 1e-06))  36.7 us
  transfers between devices with their start and end apart: 7, of which 6 were waited for; matrix products, arithmetic and copies ran while one was open for 12% of the time, Pallas kernels for 0%

commit v1 on v0

--- a/solution.py
+++ b/solution.py
@@ -51,7 +51,7 @@
         state_b = state.astype(jnp.bfloat16)
         moved = jnp.dot(basis_b, state_b, preferred_element_type=jnp.float32).astype(jnp.bfloat16)
         partial_sum = term_partial(left_ops, right_ops, moved)
-        term_total = lax.psum(partial_sum, "term")
+        term_total = jnp.sum(lax.all_gather(partial_sum, "term"), axis=0)
         applied = lax.dot_general(
             basis_wide, term_total, (((0,), (0,)), ((), ())), precision=lax.Precision.HIGHEST
         )

time: 1200 us -> 1150 us (0.958)
  waiting for transfers between devices: 884 us -> 826 us
  other arithmetic: 61.5 us -> 82.2 us
  local copies, waits for them, and re-layouts: 35.8 us -> 22.1 us
    psum x4 -> x0, waiting for transfers between devices: 428 us -> none  [half_sweep(): term_total = lax.psum(partial_sum, 'term')]
    all_gather x0 -> x4, waiting for transfers between devices: none -> 369 us  [half_sweep(): term_total = jnp.sum(lax.all_gather(partial_sum, 'term'), axis=0)]
    reduce_sum x0 -> x4, other arithmetic: none -> 22 us  [half_sweep(): term_total = jnp.sum(lax.all_gather(partial_sum, 'term'), axis=0)]
    unnamed x30 -> x28, local copies, waits for them, and re-layouts: 21.9 us -> 9.65 us
  transfers between devices with their start and end apart: 7 -> 7, of which waited for: 6 -> 6; matrix products, arithmetic and copies ran while one was open for 12% -> 13% of each run, Pallas kernels for 0% -> 0%
where the time goes in v1:
time: 1150 us
  waiting for transfers between devices  826 us (72%)
  matrix products  174 us (15%)
  other arithmetic  82.2 us (7%)
  local copies, waits for them, and re-layouts  22.1 us (2%)
  loops' own time  20.8 us (2%)
  between operations  18.7 us (2%)
    all_gather x2, waiting for transfers between devices, prefix(): gathered = lax.all_gather(part, axis)  457 us
    all_gather x4, waiting for transfers between devices, half_sweep(): term_total = jnp.sum(lax.all_gather(partial_sum, 'term'), axis=0)  369 us
    dot_general x31, matrix products, combine_env(): jnp.dot(earlier, later, precision=lax.Precision.HIGHEST)  129 us
    mul x33, other arithmetic, normed(): return block * (target / jnp.sqrt(jnp.sum(block * block) + 1e-06))  36.9 us
  transfers between devices with their start and end apart: 7, of which 6 were waited for; matrix products, arithmetic and copies ran while one was open for 13% of the time, Pallas kernels for 0%

profile of v1, /device:TPU:2, one launch (start us, length us, event | category | flops | bytes accessed | tf_op | source)
XLA Modules:
  0.0 1148.2 jit_solution(4828620765279658668)
XLA Ops:
  6.5 2.7 copy.19
  20.3 227.8 %all-gather.11.cloned.1.call-done = f32[32,512,512]{2,1,0:T(8,128)} async-done(((f32[1,512,512]{2,1,0:T(8,128)}), f32[32,512,512]{2,1,0:T(8,128)}) %all-gather.11.cloned.1.call-update) | async-done | bytes 33554448 | tf_op jit(solution)/shard_map/all_gather | solution.py:13
  248.2 47.2 %while.22 = (s32[]{:T(128)}, f32[512,512]{0,1:T(8,128)}, s32[]{:T(128)}, f32[32,512,512]{2,1,0:T(8,128)}, s32[]{:T(128)}, /*index=5*/s32[]{:T(128)}, s32[]{:T(128)}, f32[]{:T(128)}, f32[]{:T(128)}) while((s32[]{:T(128)}, f32[512,512]{0,1:T(8,128)}, s32[]{:T(128)}, f32[32,512,512]{2,1,0:T(8,128)}, s32[]{:T(128)}, /*index=5*/s32[]{:T(128)}, ...), condition=%wide.region_4.5_spmd, body=%wide.region_2.4_spmd.sunk | while | flops 1611399168 | bytes 5243051 | solution.py:20
  248.2 4.2 multiply_reduce_fusion.9
  254.1 4.2 multiply_reduce_fusion.9
  260.0 4.2 multiply_reduce_fusion.9
  265.9 4.2 multiply_reduce_fusion.9
  271.8 4.2 multiply_reduce_fusion.9
  277.7 4.2 multiply_reduce_fusion.9
  283.6 4.2 multiply_reduce_fusion.9
  289.5 4.2 multiply_reduce_fusion.9
  297.5 2.6 fusion.78
  300.1 5.2 fusion.48
  307.0 2.7 copy.21
  311.0 178.7 %all-gather.15.cloned.1.call-done = f32[4096,512]{1,0:T(8,128)} async-done(((f32[512,512]{1,0:T(8,128)}), f32[4096,512]{1,0:T(8,128)}) %all-gather.15.cloned.1.call-update) | async-done | bytes 8388624 | tf_op jit(solution)/shard_map/all_gather | solution.py:54
  489.6 5.6 reduce_sum.131
  495.3 4.5 multiply_reduce_fusion.5
  502.1 4.9 fusion.55
  507.1 2.6 copy.25
  512.4 2.4 fusion.83
  515.0 44.7 %all-gather.17.cloned.1.call-done = f32[4096,512]{1,0:T(8,128)} async-done(((f32[512,512]{1,0:T(8,128)}), f32[4096,512]{1,0:T(8,128)}) %all-gather.17.cloned.1.call-update) | async-done | bytes 8388624 | tf_op jit(solution)/shard_map/all_gather | solution.py:54
  559.7 5.5 reduce_sum.133
  565.1 4.6 multiply_reduce_fusion.4
  572.5 3.5 collective-permute-start
  576.0 229.1 %all-gather.13.cloned.1.call-done = f32[32,512,512]{2,1,0:T(8,128)} async-done(((f32[1,512,512]{2,1,0:T(8,128)}), f32[32,512,512]{2,1,0:T(8,128)}) %all-gather.13.cloned.1.call-update) | async-done | bytes 33554448 | tf_op jit(solution)/shard_map/all_gather | solution.py:13
  805.1 135.6 %while.23 = (s32[]{:T(128)}, f32[512,512]{0,1:T(8,128)}, s32[]{:T(128)}, f32[32,512,512]{2,1,0:T(8,128)}, s32[]{:T(128)}, /*index=5*/s32[]{:T(128)}, s32[]{:T(128)}, s32[]{:T(128)}, f32[]{:T(128)}, f32[]{:T(128)}) while((s32[]{:T(128)}, f32[512,512]{0,1:T(8,128)}, s32[]{:T(128)}, f32[32,512,512]{2,1,0:T(8,128)}, s32[]{:T(128)}, ...), condition=%wide.region_13.14_spmd, body=%wide.region_11.13_spmd.sunk | while | flops 1611399168 | bytes 5243071 | solution.py:20
  805.1 4.1 multiply_reduce_fusion.10
  811.0 4.1 multiply_reduce_fusion.10
  816.9 4.1 multiply_reduce_fusion.10
  822.8 4.1 multiply_reduce_fusion.10
  828.7 4.1 multiply_reduce_fusion.10
  834.6 4.1 multiply_reduce_fusion.10
  840.5 4.1 multiply_reduce_fusion.10
  846.4 4.1 multiply_reduce_fusion.10
  852.3 4.1 multiply_reduce_fusion.10
  858.2 4.1 multiply_reduce_fusion.10
  864.1 4.1 multiply_reduce_fusion.10
  870.0 4.1 multiply_reduce_fusion.10
  875.9 4.1 multiply_reduce_fusion.10
  881.8 4.1 multiply_reduce_fusion.10
  887.7 4.1 multiply_reduce_fusion.10
  893.6 4.1 multiply_reduce_fusion.10
  899.5 4.1 multiply_reduce_fusion.10
  905.4 4.1 multiply_reduce_fusion.10
  911.2 4.1 multiply_reduce_fusion.10
  917.1 4.1 multiply_reduce_fusion.10
  923.0 4.1 multiply_reduce_fusion.10
  928.9 4.1 multiply_reduce_fusion.10
  934.8 4.1 multiply_reduce_fusion.10
  945.7 2.4 fusion.80
  948.1 5.1 fusion.62
  953.5 94.3 %all-gather.19.cloned.1.call-done = f32[4096,512]{1,0:T(8,128)} async-done(((f32[512,512]{1,0:T(8,128)}), f32[4096,512]{1,0:T(8,128)}) %all-gather.19.cloned.1.call-update) | async-done | bytes 8388624 | tf_op jit(solution)/shard_map/all_gather | solution.py:54
  1047.8 5.5 reduce_sum.137
  1053.2 3.5 fusion.110
  1056.7 2.5 copy.26
  1059.3 3.1 multiply_reduce_fusion.2
  1062.9 2.7 fusion.81
  1065.6 5.1 fusion.69
  1072.0 51.3 %all-gather.21.cloned.1.call-done = f32[4096,512]{1,0:T(8,128)} async-done(((f32[512,512]{1,0:T(8,128)}), f32[4096,512]{1,0:T(8,128)}) %all-gather.21.cloned.1.call-update) | async-done | bytes 8388624 | tf_op jit(solution)/shard_map/all_gather | solution.py:54
  1123.3 5.5 reduce_sum.139
  1128.8 3.3 fusion.111
  1132.1 2.7 copy.27
  1134.8 2.2 fusion.93
  1137.7 2.3 fusion.85
  (86 shorter events, 61.6 us)
Async XLA Ops:
  6.5 293.6 %copy-start = (bf16[1,4,512,512]{3,2,1,0:T(8,128)(2,1)S(1)}, bf16[1,4,512,512]{3,2,1,0:T(8,128)(2,1)}, u32[]{:S(2)}) copy-start(bf16[1,4,512,512]{3,2,1,0:T(8,128)(2,1)} %param.11) | copy-start | bytes 6291460
  6.5 5.4 copy-start.9
  6.5 241.6 %all-gather.11.cloned.1.call-start = ((), (), s32[]{:S(2)}) async-start(), calls=%async_computation | async-start | bytes 34603008 | tf_op jit(solution)/shard_map/all_gather | solution.py:13
  13.1 1.6 copy-start.11
  13.1 476.6 %all-gather.15.cloned.1.call-start = ((), (), s32[]{:S(2)}) async-start(), calls=%async_computation.2 | async-start | bytes 9437184 | tf_op jit(solution)/shard_map/all_gather | solution.py:54
  14.7 5.6 copy-start.2
  18.4 1.0 copy-start.1
  296.7 0.8 copy-start.4
  300.1 5.3 copy-start.3
  305.4 254.3 %all-gather.17.cloned.1.call-start = ((), (), s32[]{:S(2)}) async-start(), calls=%async_computation.3 | async-start | bytes 9437184 | tf_op jit(solution)/shard_map/all_gather | solution.py:54
  307.0 2.7 copy-start.10
  489.6 5.6 copy-start.5
  507.0 298.1 %all-gather.13.cloned.1.call-start = ((), (), s32[]{:S(2)}) async-start(), calls=%async_computation.1 | async-start | bytes 34603008 | tf_op jit(solution)/shard_map/all_gather | solution.py:13
  514.8 533.0 %all-gather.19.cloned.1.call-start = ((), (), s32[]{:S(2)}) async-start(), calls=%async_computation.4 | async-start | bytes 9437184 | tf_op jit(solution)/shard_map/all_gather | solution.py:54
  572.5 370.4 %collective-permute-start = (bf16[512,512]{1,0:T(8,128)(2,1)}, bf16[512,512]{1,0:T(8,128)(2,1)}, u32[]{:S(2)}, u32[]{:S(2)}) collective-permute-start(bf16[512,512]{1,0:T(8,128)(2,1)} %multiply_convert_fusion.2), channel_id=1, source_target_pairs={{0,8},{8,16},{16,24},{24,32},{32,40},{40,48},{48,56},{56,64},{64,7... | collective-permute-start | bytes 1572872 | tf_op jit(solution)/shard_map/ppermute | solution.py:26
  940.7 2.2 copy-start.7
  953.2 170.1 %all-gather.21.cloned.1.call-start = ((), (), s32[]{:S(2)}) async-start(), calls=%async_computation.5 | async-start | bytes 9437184 | tf_op jit(solution)/shard_map/all_gather | solution.py:54
  1123.3 5.5 copy-start.6
  1132.1 2.7 copy-start.8
Sparse Core Ops, SparseCore 0:
  13.2 234.9 all-gather.10
  305.5 184.0 all-gather.14
  507.2 52.4 all-gather.16
  562.1 242.9 all-gather.12
  953.3 94.4 all-gather.18
  1070.8 52.4 all-gather.20
